TPU v7x, 32 devices: a whole 2x2x4 slice. The times are simulated.
32 devices in a mesh: fine: 4 (over z), coarse: 2 (over y), comp: 4 (over x, core).
Axes of the slice: x: 2, y: 2, z: 4, core: 2. Of those that a mesh axis runs over, the one named last changes fastest.
Arguments:
- a_vals: bfloat16 [384, 64, 448], P(('fine', 'coarse', 'comp')), may hold values from -0.25 to 0.25
- a_cols: int32 [384, 7], P(('fine', 'coarse', 'comp')), may hold values from 0 to 27, as said below
- p_vals: bfloat16 [384, 64, 256], P(('fine', 'coarse', 'comp')), may hold values from -1 to 1
- p_cols: int32 [384, 4], P(('fine', 'coarse', 'comp')), may hold values from 0 to 7, as said below
- gp_cols: int32 [512, 4], P(('fine', 'coarse', 'comp')), may hold values from 0 to 15, as said below
- send_list: int32 [512], P(('fine', 'coarse', 'comp')), may hold values from 0 to 11
Outputs:
- coarse_op: float32 [4, 512, 4, 1024], P('fine', 'coarse', 'comp')
Inputs may be any that keep to these rules, and one draw needn't show every extreme that they name: `a_cols`: A value e below 12 names local row e of the same device, a value 12 + s names ghost slot s; the first entry of each row is the row itself, and every ghost slot of a device is named by at least one entry of its rows. `p_cols`: the 4 entries of a row are distinct. `gp_cols`: the 4 entries of a row are distinct.
All inputs are finite; a program needn't handle non-finite values.
Results may differ from a plain program's by a relative error of at most 0.0029.
Values may be sent and summed in bfloat16 or wider, within the bound.
A program may use at most 64 MiB of HBM per device.

v0:
```python
import jax
import jax.numpy as jnp
from jax import lax
from jax.sharding import PartitionSpec as P

NC = 8
EXT = 8


def local_terms(a_rows, a_index, p_rows, p_index, ghosts, g_index):
    block_rows = a_rows.shape[0]
    block_size = a_rows.shape[1]
    pick_count = p_index.shape[1]
    link_count = a_index.shape[1]
    columns_all = NC + EXT
    sources = jnp.concatenate([p_rows, ghosts], axis=0)
    source_cols = jnp.concatenate([p_index, g_index], axis=0)
    fetched = jnp.take(sources, a_index, axis=0)
    fetched_cols = jnp.take(source_cols, a_index, axis=0)
    column_ids = jnp.arange(columns_all, dtype=jnp.int32)
    placing = (fetched_cols[:, :, :, None] == column_ids[None, None, None, :]).astype(jnp.float32)
    a_split = a_rows.reshape(block_rows, block_size, link_count, block_size)
    terms = jnp.einsum("riam,ramn->rain", a_split, fetched, preferred_element_type=jnp.float32)
    terms = terms.reshape(block_rows, block_size, link_count, pick_count, block_size)
    applied = jnp.einsum("rakc,riakj->ricj", placing, terms, precision=lax.Precision.HIGHEST)
    prod_rows = applied.astype(jnp.bfloat16).reshape(
        block_rows * block_size, columns_all * block_size
    )
    own_rows = p_rows.reshape(block_rows, block_size, pick_count, block_size)
    owned_ids = jnp.arange(NC, dtype=jnp.int32)
    spread = jnp.zeros((block_rows, block_size, NC, block_size), jnp.bfloat16)
    for pick in range(pick_count):
        hits = p_index[:, pick, None] == owned_ids[None, :]
        spread = jnp.where(hits[:, None, :, None], own_rows[:, :, pick, None, :], spread)
    spread = spread.reshape(block_rows * block_size, NC * block_size)
    return (spread, prod_rows)


def contract(spread, prod_rows):
    return lax.dot_general(
        spread, prod_rows, (((0,), (0,)), ((), ())), preferred_element_type=jnp.float32
    )


def on_device(a_vals, a_cols, p_vals, p_cols, gp_cols, send_list):
    outgoing = jnp.take(p_vals, send_list, axis=0)
    arrived = lax.all_to_all(outgoing, ("fine", "comp"), split_axis=0, concat_axis=0, tiled=True)
    spread, prod_rows = local_terms(a_vals, a_cols, p_vals, p_cols, arrived, gp_cols)
    owned = lax.psum_scatter(contract(spread, prod_rows), "coarse", scatter_dimension=0, tiled=True)
    return owned.reshape((1, owned.shape[0], 1, owned.shape[1]))


def solution(mesh):
    placed = (
        P(("fine", "coarse", "comp"), None, None),
        P(("fine", "coarse", "comp"), None),
        P(("fine", "coarse", "comp"), None, None),
        P(("fine", "coarse", "comp"), None),
        P(("fine", "coarse", "comp"), None),
        P(("fine", "coarse", "comp")),
    )
    return jax.shard_map(
        on_device,
        mesh=mesh,
        in_specs=placed,
        out_specs=P("fine", "coarse", "comp", None),
        check_vma=False,
    )
```

profile of v0, /device:TPU:0, one launch (start us, length us, event | category | flops | bytes accessed | tf_op | source)
XLA Modules:
  0.0 109.3 jit_solution(4293900325536399541)
XLA Ops:
  6.5 0.0 copy-start
  6.5 0.7 compare_select_fusion.1
  7.2 0.7 compare_and_fusion.1
  7.9 1.6 %gather_fusion = bf16[16,64,256]{2,1,0:T(8,128)(2,1)S(1)} fusion(bf16[12,64,256]{2,1,0:T(8,128)(2,1)} %param.8, s32[1024]{0:T(1024)S(1)} %pad_clamp_fusion.1), kind=kCustom, calls=%fused_computation | custom fusion | bytes 1048640 | tf_op jit(solution)/shard_map/jit(_take)/gather | solution.py:46
  9.5 0.9 broadcast_select_fusion
  10.4 7.4 %all-to-all-start = ((bf16[16,64,256]{2,1,0:T(8,128)(2,1)}), bf16[16,64,256]{2,1,0:T(8,128)(2,1)S(1)}, u32[]{:S(2)}, u32[]{:S(2)}) async-start(bf16[16,64,256]{2,1,0:T(8,128)(2,1)} %broadcast_select_fusion), calls=%async_computation | async-start | bytes 1048576 | tf_op jit(solution)/shard_map/all_to_all | solution.py:47
  17.8 0.0 copy-start.2
  17.8 0.0 reduce-scatter.2.cloned.1.call-start
  17.8 0.0 copy-done
  17.9 0.3 reshape.149
  18.2 1.7 %fusion.13 = (bf16[12,64,1,64]{3,2,1,0:T(2,128)(2,1)S(1)}, bf16[12,64,1,64]{3,2,1,0:T(2,128)(2,1)S(1)}, bf16[12,64,1,64]{3,2,1,0:T(2,128)(2,1)S(1)}, bf16[12,64,1,64]{3,2,1,0:T(2,128)(2,1)S(1)}) fusion(bf16[12,64,4,64]{3,2,1,0:T(4,128)(2,1)S(1)} %reshape.149), kind=kLoop, calls=%fused_computation.38 | loop fusion | bytes 786432 | tf_op jit(solution)/shard_map/slice | solution.py:34
  19.9 0.0 copy-done.2
  19.9 0.1 copy_bitcast_fusion.2
  20.0 0.1 copy_bitcast_fusion
  20.0 0.1 iota_compare_fusion.3
  20.1 0.1 iota_compare_fusion.1
  20.2 0.0 copy-start.1
  20.2 0.9 select_select_fusion
  21.1 0.0 copy-start.3
  21.1 1.7 %select_n.79 = bf16[768,512]{1,0:T(8,128)(2,1)} reshape(bf16[12,64,8,64]{3,2,1,0:T(8,128)(2,1)S(1)} %select_select_fusion) | data formatting | bytes 1572864 | tf_op jit(solution)/shard_map/jit(_where)/select_n | solution.py:34
  22.8 0.0 copy-done.1
  22.8 0.1 copy.36
  22.9 0.1 reshape.164
  23.0 0.1 copy.35
  23.1 2.5 %reshape.150 = bf16[12,64,7,64]{3,2,1,0:T(8,128)(2,1)S(1)} reshape(bf16[12,64,448]{2,1,0:T(8,128)(2,1)} %param.6) | data formatting | bytes 1376256 | tf_op jit(solution)/shard_map/reshape | solution.py:22
  25.6 0.0 copy-done.3
  25.6 0.1 pad_add_fusion
  25.7 0.1 copy.39
  25.8 0.6 gather_fusion.2
  26.4 0.1 copy.40
  26.5 0.1 reshape.171
  26.6 0.2 copy.41
  26.8 5.5 %all-to-all-done = bf16[16,64,256]{2,1,0:T(8,128)(2,1)S(1)} async-done(((bf16[16,64,256]{2,1,0:T(8,128)(2,1)}), bf16[16,64,256]{2,1,0:T(8,128)(2,1)S(1)}, u32[]{:S(2)}, u32[]{:S(2)}) %all-to-all-start) | async-done | bytes 524320 | tf_op jit(solution)/shard_map/all_to_all | solution.py:47
  32.3 0.1 pad_maximum_fusion
  32.3 2.4 %gather_fusion.1 = bf16[84,64,256]{2,1,0:T(8,128)(2,1)} fusion(bf16[28,64,256]{2,1,0:T(8,128)(2,1)S(1)} %pad_maximum_fusion, s32[1024]{0:T(1024)S(1)} %pad_clamp_fusion), kind=kCustom, calls=%fused_computation.1 | custom fusion | bytes 5505360 | tf_op jit(solution)/shard_map/jit(_take)/gather | solution.py:18
  34.8 5.1 %fusion.4 = f32[12,7,64,256]{3,2,1,0:T(8,128)} fusion(bf16[12,7,64,256]{3,2,1,0:T(8,128)(2,1)} %bitcast.43, pred[12,7]{1,0:T(8,128)(4,1)S(1)} %copy.35, bf16[12,64,7,64]{3,2,1,0:T(8,128)(2,1)S(1)} %reshape.150), kind=kOutput, calls=%fused_computation.8 | convolution fusion | flops 177537024 | bytes 8945748 | tf_op jit(solution)/shard_map/riam,ramn->rain/dot_general | solution.py:23
  39.9 10.1 %reshape.151 = f32[12,64,7,4,64]{4,3,2,1,0:T(4,128)} reshape(f32[12,7,64,256]{3,2,1,0:T(8,128)} %fusion.4) | data formatting | bytes 11010048 | tf_op jit(solution)/shard_map/reshape | solution.py:24
  50.0 10.6 %fusion = bf16[12,64,16,64]{3,2,1,0:T(8,128)(2,1)S(1)} fusion(f32[12,64,7,4,64]{4,3,2,1,0:T(4,128)} %reshape.151, s32[12,7,4]{2,1,0:T(8,128)S(1)} %copy.41), kind=kOutput, calls=%fused_computation.4 | convolution fusion | flops 265032960 | bytes 7079232 | tf_op jit(solution)/shard_map/rakc,riakj->ricj/dot_general | solution.py:25
  60.6 3.2 %reshape.152 = bf16[768,1024]{1,0:T(8,128)(2,1)} reshape(bf16[12,64,16,64]{3,2,1,0:T(8,128)(2,1)S(1)} %fusion) | data formatting | bytes 3145728 | tf_op jit(solution)/shard_map/reshape | solution.py:26
  63.8 4.0 %fusion.14 = f32[512,1024]{1,0:T(8,128)} fusion(bf16[768,512]{1,0:T(8,128)(2,1)} %select_n.79, bf16[768,1024]{1,0:T(8,128)(2,1)} %reshape.152), kind=kOutput, calls=%fused_computation.39 | convolution fusion | flops 805306368 | bytes 4456448 | tf_op jit(solution)/shard_map/dot_general | solution.py:40
  67.8 0.0 reduce-scatter.2.cloned.1.call-update
  67.8 31.4 %reduce-scatter.2.cloned.1.call-done = f32[256,1024]{1,0:T(8,128)} async-done(((f32[512,1024]{1,0:T(8,128)}), f32[256,1024]{1,0:T(8,128)}) %reduce-scatter.2.cloned.1.call-update) | async-done | bytes 1048592 | tf_op jit(solution)/shard_map/reduce_scatter | solution.py:49
  99.2 3.3 %copy.42 = f32[1,256,1,1024]{3,2,1,0:T(1,128)} copy(f32[1,256,1,1024]{3,1,2,0:T(8,128)} %bitcast.44) | data formatting | bytes 2097152 | tf_op jit(solution)/shard_map/reshape | solution.py:50
  (6 shorter events, 0.0 us)
Async XLA Ops:
  6.5 11.3 %copy-start = (bf16[12,64,256]{2,1,0:T(8,128)(2,1)S(1)}, bf16[12,64,256]{2,1,0:T(8,128)(2,1)}, u32[]{:S(2)}) copy-start(bf16[12,64,256]{2,1,0:T(8,128)(2,1)} %param.8) | copy-start | bytes 1179652
  10.4 21.8 %all-to-all-start = ((bf16[16,64,256]{2,1,0:T(8,128)(2,1)}), bf16[16,64,256]{2,1,0:T(8,128)(2,1)S(1)}, u32[]{:S(2)}, u32[]{:S(2)}) async-start(bf16[16,64,256]{2,1,0:T(8,128)(2,1)} %broadcast_select_fusion), calls=%async_computation | async-start | bytes 1048576 | tf_op jit(solution)/shard_map/all_to_all | solution.py:47
  17.8 2.1 %copy-start.2 = (s32[12,4]{0,1:T(4,128)S(1)}, s32[12,4]{0,1:T(4,128)}, u32[]{:S(2)}) copy-start(s32[12,4]{0,1:T(4,128)} %param.9) | copy-start | bytes 580
  17.8 81.4 %reduce-scatter.2.cloned.1.call-start = ((), (), s32[]{:S(2)}) async-start(), calls=%async_computation.2 | async-start | bytes 3145728 | tf_op jit(solution)/shard_map/reduce_scatter | solution.py:49
  20.2 2.6 %copy-start.1 = (s32[12,7]{0,1:T(8,128)S(1)}, s32[12,7]{0,1:T(8,128)}, u32[]{:S(2)}) copy-start(s32[12,7]{0,1:T(8,128)} %param.7) | copy-start | bytes 1012
  21.1 4.5 %copy-start.3 = (s32[16,4]{0,1:T(4,128)S(1)}, s32[16,4]{0,1:T(4,128)}, u32[]{:S(2)}) copy-start(s32[16,4]{0,1:T(4,128)} %param.10) | copy-start | bytes 772
Sparse Core Ops, SparseCore 0:
  67.9 31.2 reduce-scatter.1
where the time goes:
time: 110 us; the launch traced here: 109 us
  waiting for transfers between devices  36.9 us (34%)
  local copies, waits for them, and re-layouts  28.2 us (26%)
  matrix products  19.7 us (18%)
  between operations  13.5 us (12%)
  starting transfers between devices  7.4 us (7%)
  other arithmetic  3.55 us (3%)
    reduce_scatter x1, waiting for transfers between devices, on_device(): lax.psum_scatter(contract(spread, prod_rows), 'coarse', scatter_dimension...  31.4 us
    dot_general x1, matrix products, local_terms(): jnp.einsum('rakc,riakj->ricj', placing, terms, precision=lax.Precision.HI...  10.6 us
    reshape x1, local copies, waits for them, and re-layouts, local_terms(): terms.reshape(block_rows, block_size, link_count, pick_count, block_size)  10.1 us
    all_to_all x1, starting transfers between devices, on_device(): lax.all_to_all(outgoing, ('fine', 'comp'), split_axis=0, concat_axis=0, t...  7.36 us
    all_to_all x1, waiting for transfers between devices, on_device(): lax.all_to_all(outgoing, ('fine', 'comp'), split_axis=0, concat_axis=0, t...  5.5 us
    dot_general x1, matrix products, local_terms(): jnp.einsum('riam,ramn->rain', a_split, fetched, preferred_element_type=jn...  5.08 us
    dot_general x1, matrix products, contract(): lax.dot_general(spread, prod_rows, (((0,), (0,)), ((), ())), preferred_el...  3.98 us
    reshape x1, local copies, waits for them, and re-layouts, on_device(): return owned.reshape((1, owned.shape[0], 1, owned.shape[1]))  3.27 us
  transfers between devices with their start and end apart: 2, of which 2 were waited for; matrix products, arithmetic and copies ran while one was open for 8% of the time, Pallas kernels for 0%

commit v1 on v0

v1 whole, which is shorter than its diff:
```python
import functools

import jax
import jax.numpy as jnp
from jax import lax
from jax.experimental import pallas as pl
from jax.experimental.pallas import tpu as pltpu
from jax.sharding import PartitionSpec as P

NC = 8
EXT = 8
MESH = pl.DeviceIdType.MESH


def doubled(pair, low):
    turned = pltpu.roll(pair, 64, 1)
    return jnp.where(low, pair, turned), jnp.where(low, turned, pair)


def placed(tiles, ids, columns):
    out = jnp.zeros(tiles[0].shape, jnp.float32)
    for tile, column in zip(tiles, columns):
        out = jnp.where(ids == column, tile, out)
    return out


def kernel(
    shape, a_ref, p_ref, a_cols, p_cols, gp_cols, send_list, out_ref,
    staging, sources, terms, spread, total, prod, outgoing, incoming,
    send_sem, recv_sem, part_send, part_recv,
):
    n_fine, n_coarse, n_comp, per_peer = shape
    block_rows, block, _ = a_ref.shape
    links = a_cols.shape[1]
    picks = p_cols.shape[1]
    group = n_comp * per_peer
    rows = NC * block // n_coarse
    columns = (NC + EXT) * block
    strips = columns // 256
    f, c, m = lax.axis_index("fine"), lax.axis_index("coarse"), lax.axis_index("comp")
    me = f * n_comp + m

    barrier = pltpu.get_barrier_semaphore()
    far = [(df, dm) for t in range(n_fine) for df in [(n_fine // 2 + t) % n_fine]
           for dm in range(n_comp) if df or dm]
    for df, dm in far:
        pl.semaphore_signal(
            barrier, inc=1, device_id_type=MESH,
            device_id=(lax.rem(f + df, n_fine), c, lax.rem(m + dm, n_comp)),
        )
    for dc in range(1, n_coarse):
        pl.semaphore_signal(
            barrier, inc=1, device_id_type=MESH, device_id=(f, lax.rem(c + dc, n_coarse), m)
        )

    def stage(slot, carry):
        staging[slot] = p_ref[send_list[slot]]
        return carry

    lax.fori_loop(0, n_fine * group, stage, 0)
    pl.semaphore_wait(barrier, len(far) + n_coarse - 1)

    def ghost_copy(peer_f, peer_m, to_slot):
        peer = peer_f * n_comp + peer_m
        return pltpu.make_async_remote_copy(
            src_ref=staging.at[pl.ds(peer * per_peer, per_peer)],
            dst_ref=sources.at[pl.ds(block_rows + to_slot * per_peer, per_peer)],
            send_sem=send_sem.at[peer],
            recv_sem=recv_sem.at[to_slot],
            device_id=(peer_f, c, peer_m),
            device_id_type=MESH,
        )

    for df, dm in far:
        ghost_copy(lax.rem(f + df, n_fine), lax.rem(m + dm, n_comp), me).start()
    for g in range(per_peer):
        sources[block_rows + me * per_peer + g] = staging[me * per_peer + g]

    lane = lax.broadcasted_iota(jnp.int32, (block, 128), 1)
    low = lane < block
    upper = jnp.where(low, 0, 1)

    def split_tiles(value, low):
        tiles = []
        for k in range(picks // 2):
            tiles.extend(doubled(value[:, k * 128:(k + 1) * 128].astype(jnp.float32), low))
        return tiles

    def local_pair(pair, carry):
        halves = []
        for side in range(2):
            row = pair * 2 + side
            value = p_ref[row]
            sources[row] = value
            tiles = split_tiles(value, low)
            ids = [p_cols[row, k] for k in range(picks)]
            halves.append([placed(tiles, upper + 2 * i, ids) for i in range(NC // 2)])
        where = pl.ds(pl.multiple_of(pair * 128, 128), 128)
        for i in range(NC // 2):
            both = jnp.concatenate([halves[0][i], halves[1][i]], axis=0)
            spread[i * 128:(i + 1) * 128, where] = both.T.astype(jnp.bfloat16)
        return carry

    lax.fori_loop(0, block_rows // 2, local_pair, 0)

    for df, dm in reversed(far):
        peer_f, peer_m = lax.rem(f + df, n_fine), lax.rem(m + dm, n_comp)
        ghost_copy(peer_f, peer_m, peer_f * n_comp + peer_m).wait_recv()

    half = block // 2
    low_half = lax.broadcasted_iota(jnp.int32, (half, 128), 1) < block
    upper_half = jnp.where(low_half, 0, 1)

    def fine_row(row, side):
        entries = [a_cols[row, a] for a in range(links)]
        for a in range(links):
            term = jnp.dot(
                a_ref[row, :, a * block:(a + 1) * block], sources[entries[a]],
                preferred_element_type=jnp.float32,
            )
            for h in range(picks // 2):
                terms[side, h, pl.ds(a * block, block), :] = term[:, h * 128:(h + 1) * 128]
        ids = [
            [
                jnp.where(
                    e < block_rows,
                    p_cols[jnp.minimum(e, block_rows - 1), k],
                    gp_cols[jnp.maximum(e - block_rows, 0), k],
                )
                for k in range(picks)
            ]
            for e in entries
        ]
        for part in range(2):
            sums = [None] * (columns // 128)
            for a in range(links):
                tiles = []
                for h in range(picks // 2):
                    tiles.extend(doubled(
                        terms[side, h, pl.ds(part * half * links + a, half, stride=links), :], low_half
                    ))
                for j in range(columns // 128):
                    here = placed(tiles, upper_half + 2 * j, ids[a])
                    sums[j] = here if sums[j] is None else sums[j] + here
            for j in range(columns // 128):
                prod[pl.ds(row * block + part * half, half), j * 128:(j + 1) * 128] = sums[j].astype(jnp.bfloat16)

    def fine_pair(pair, carry):
        for side in range(2):
            fine_row(pair * 2 + side, side)
        return carry

    lax.fori_loop(0, block_rows // 2, fine_pair, 0)

    def part_copy(dc, strip):
        return pltpu.make_async_remote_copy(
            src_ref=outgoing.at[dc - 1, strip],
            dst_ref=incoming.at[dc - 1, strip],
            send_sem=part_send.at[dc - 1, strip],
            recv_sem=part_recv.at[dc - 1, strip],
            device_id=(f, lax.rem(c + dc, n_coarse), m),
            device_id_type=MESH,
        )

    def contract(owner, at):
        mine = pl.ds(pl.multiple_of(owner * rows, rows), rows)
        return jnp.dot(spread[mine, :], prod[:, at], preferred_element_type=jnp.float32)

    def finish(strip, carry):
        at = pl.ds(pl.multiple_of(strip * 256, 256), 256)
        for dc in range(1, n_coarse):
            outgoing[dc - 1, strip] = contract(lax.rem(c + dc, n_coarse), at).astype(jnp.bfloat16)
            part_copy(dc, strip).start()
        return carry

    lax.fori_loop(0, strips, finish, 0)

    def own(strip, carry):
        at = pl.ds(pl.multiple_of(strip * 256, 256), 256)
        total[:, at] = contract(c, at)
        return carry

    lax.fori_loop(0, strips, own, 0)

    for strip in range(strips):
        for dc in range(1, n_coarse):
            part_copy(dc, strip).wait_recv()
        for half in range(2):
            j = strip * 2 + half
            value = total[:, j * 128:(j + 1) * 128]
            for dc in range(1, n_coarse):
                value = value + incoming[dc - 1, strip, :, half * 128:(half + 1) * 128].astype(jnp.float32)
            out_ref[pl.ds(j, rows, stride=columns // 128), :] = value

    for dc in range(1, n_coarse):
        for strip in range(strips):
            part_copy(dc, strip).wait_send()
    for df, dm in far:
        ghost_copy(lax.rem(f + df, n_fine), lax.rem(m + dm, n_comp), me).wait_send()


def on_device(shape, a_vals, a_cols, p_vals, p_cols, gp_cols, send_list):
    n_fine, n_coarse, n_comp, per_peer = shape
    block_rows, block, _ = a_vals.shape
    width = p_vals.shape[2]
    slots = gp_cols.shape[0]
    links = a_cols.shape[1]
    depth = block_rows * block
    columns = (NC + EXT) * block
    rows = NC * block // n_coarse
    strips = columns // 256
    peers = n_fine * n_comp
    vmem = pl.BlockSpec(memory_space=pltpu.VMEM)
    smem = pl.BlockSpec(memory_space=pltpu.SMEM)
    owned = pl.pallas_call(
        functools.partial(kernel, shape),
        out_shape=jax.ShapeDtypeStruct((rows * columns // 128, 128), jnp.float32),
        in_specs=[vmem, vmem, smem, smem, smem, smem],
        out_specs=vmem,
        scratch_shapes=[
            pltpu.VMEM((slots, block, width), jnp.bfloat16),
            pltpu.VMEM((block_rows + slots, block, width), jnp.bfloat16),
            pltpu.VMEM((2, width // 128, links * block, 128), jnp.float32),
            pltpu.VMEM((NC * block, depth), jnp.bfloat16),
            pltpu.VMEM((rows, columns), jnp.float32),
            pltpu.VMEM((depth, columns), jnp.bfloat16),
            pltpu.VMEM((n_coarse - 1, strips, rows, 256), jnp.bfloat16),
            pltpu.VMEM((n_coarse - 1, strips, rows, 256), jnp.bfloat16),
            pltpu.SemaphoreType.DMA((peers,)),
            pltpu.SemaphoreType.DMA((peers,)),
            pltpu.SemaphoreType.DMA((n_coarse - 1, strips)),
            pltpu.SemaphoreType.DMA((n_coarse - 1, strips)),
        ],
        compiler_params=pltpu.CompilerParams(
            collective_id=0, has_side_effects=True, vmem_limit_bytes=52 * 1024 * 1024
        ),
    )(a_vals, p_vals, a_cols, p_cols, gp_cols, send_list)
    return owned.reshape((1, rows, 1, columns))


def solution(mesh):
    n_fine, n_coarse, n_comp = (mesh.shape[axis] for axis in ("fine", "coarse", "comp"))

    def run(a_vals, a_cols, p_vals, p_cols, gp_cols, send_list):
        per_peer = gp_cols.shape[0] // (mesh.size * n_fine * n_comp)
        shape = (n_fine, n_coarse, n_comp, per_peer)
        split = ("fine", "coarse", "comp")
        return jax.shard_map(
            functools.partial(on_device, shape),
            mesh=mesh,
            in_specs=(
                P(split, None, None), P(split, None), P(split, None, None),
                P(split, None), P(split, None), P(split),
            ),
            out_specs=P("fine", "coarse", "comp", None),
            check_vma=False,
        )(a_vals, a_cols, p_vals, p_cols, gp_cols, send_list)

    return run
```

time: 110 us -> 49 us (0.45)
  Pallas kernels: 0 us -> 41.3 us
  waiting for transfers between devices: 36.9 us -> 0 us
  local copies, waits for them, and re-layouts: 28.2 us -> 7.17 us
  matrix products: 19.7 us -> 0 us
  between operations: 13.5 us -> 0.02 us
  starting transfers between devices: 7.4 us -> 0 us
  other arithmetic: 3.55 us -> 0 us
    pallas_call x0 -> x1, Pallas kernels: none -> 41.3 us  [on_device(): pl.pallas_call(functools.partial(kernel, shape), out_shape=jax.ShapeDtype...]
    reduce_scatter x1 -> x0, waiting for transfers between devices: 31.4 us -> none  [on_device(): lax.psum_scatter(contract(spread, prod_rows), 'coarse', scatter_dimension...]
    dot_general x3 -> x0, matrix products: 19.7 us -> none  [the longest x1 10.6 us: local_terms(): jnp.einsum('rakc,riakj->ricj', placing, terms, precision=lax.Precision.HI...]
    reshape x5 -> x0, local copies, waits for them, and re-layouts: 19.4 us -> none  [the longest x1 10.1 us: local_terms(): terms.reshape(block_rows, block_size, link_count, pick_count, block_size)]
    all_to_all x1 -> x0, starting transfers between devices: 7.36 us -> none  [on_device(): lax.all_to_all(outgoing, ('fine', 'comp'), split_axis=0, concat_axis=0, t...]
    unnamed x10 -> x14, local copies, waits for them, and re-layouts: 0.15 us -> 7.17 us
    all_to_all x1 -> x0, waiting for transfers between devices: 5.5 us -> none  [on_device(): lax.all_to_all(outgoing, ('fine', 'comp'), split_axis=0, concat_axis=0, t...]
    gather x5 -> x0, local copies, waits for them, and re-layouts: 4.78 us -> none  [the longest x1 2.43 us: local_terms(): fetched = jnp.take(sources, a_index, axis=0)]
  transfers between devices with their start and end apart: 2 -> 0, of which waited for: 2 -> 0; matrix products, arithmetic and copies ran while one was open for 8% -> 0% of each run, Pallas kernels for 0% -> 0%
where the time goes in v1:
time: 49 us; the launch traced here: 48.5 us
  Pallas kernels  41.3 us (84%)
  local copies, waits for them, and re-layouts  7.17 us (15%)
    pallas_call x1, Pallas kernels, on_device(): pl.pallas_call(functools.partial(kernel, shape), out_shape=jax.ShapeDtype...  41.3 us
    unnamed x14, local copies, waits for them, and re-layouts  7.17 us

profile of v1, /device:TPU:0, one launch (start us, length us, event | category | flops | bytes accessed | tf_op | source)
XLA Modules:
  0.0 48.5 jit_solution(12627063209258491486)
XLA Ops:
  0.0 0.0 copy-start.3
  0.0 0.8 %copy.7.a_cols = s32[12,7]{1,0:T(8,128)S(1)} copy(s32[12,7]{0,1:T(8,128)} %param.7) | data formatting | bytes 672 | tf_op args[1]
  0.8 0.0 copy-done.3
  0.8 0.0 copy-start.4
  0.8 0.1 copy.8.p_cols
  0.9 0.6 %copy-done.4 = s32[16,4]{0,1:T(4,128)S(1)} copy-done((s32[16,4]{0,1:T(4,128)S(1)}, s32[16,4]{0,1:T(4,128)}, u32[]{:S(2)}) %copy-start.4) | copy-done | bytes 280
  1.5 0.0 copy-start.2
  1.5 0.1 copy.9.gp_cols
  1.6 0.6 %copy-done.2 = s32[16]{0:T(128)S(1)} copy-done((s32[16]{0:T(128)S(1)}, s32[16]{0:T(128)}, u32[]{:S(2)}) %copy-start.2) | copy-done | bytes 88
  2.1 0.0 copy-start
  2.1 1.1 %copy-done = bf16[12,64,448]{2,1,0:T(8,128)(2,1)S(1)} copy-done((bf16[12,64,448]{2,1,0:T(8,128)(2,1)S(1)}, bf16[12,64,448]{2,1,0:T(8,128)(2,1)}, u32[]{:S(2)}) %copy-start) | copy-done | bytes 688152
  3.3 0.0 copy-start.1
  3.3 1.0 %copy-done.1 = bf16[12,64,256]{2,1,0:T(8,128)(2,1)S(1)} copy-done((bf16[12,64,256]{2,1,0:T(8,128)(2,1)S(1)}, bf16[12,64,256]{2,1,0:T(8,128)(2,1)}, u32[]{:S(2)}) %copy-start.1) | copy-done | bytes 393240
  4.3 41.3 %shard_map.64 = f32[2048,128]{1,0:T(8,128)} custom-call(bf16[12,64,448]{2,1,0:T(8,128)(2,1)S(1)} %copy-done, bf16[12,64,256]{2,1,0:T(8,128)(2,1)S(1)} %copy-done.1, s32[12,7]{1,0:T(8,128)S(1)} %copy.7.a_cols, s32[12,4]{1,0:T(8,128)S(1)} %copy.8.p_cols, s32[16,4]{1,0:T(8,128)S(1)} %copy.9.gp_cols, s32[16]{0:T(128)S(1)} %copy-done.2), custom_call_target="tpu_custom_call" | custom-call | tf_op jit(solution)/shard_map/pallas_call | solution.py:215
  45.6 2.9 %copy.12 = f32[1,256,1,1024]{3,2,1,0:T(1,128)} copy(f32[1,256,1,1024]{3,2,1,0:T(1,128)} %bitcast.1) | data formatting | bytes 2097152
Async XLA Ops:
  0.0 0.8 %copy-start.3 = (s32[12,4]{0,1:T(4,128)S(1)}, s32[12,4]{0,1:T(4,128)}, u32[]{:S(2)}) copy-start(s32[12,4]{0,1:T(4,128)} %param.9) | copy-start | bytes 580
  0.8 0.7 %copy-start.4 = (s32[16,4]{0,1:T(4,128)S(1)}, s32[16,4]{0,1:T(4,128)}, u32[]{:S(2)}) copy-start(s32[16,4]{0,1:T(4,128)} %param.10) | copy-start | bytes 772
  1.5 0.7 %copy-start.2 = (s32[16]{0:T(128)S(1)}, s32[16]{0:T(128)}, u32[]{:S(2)}) copy-start(s32[16]{0:T(128)} %send_list.1) | copy-start | bytes 196
  2.1 1.1 %copy-start = (bf16[12,64,448]{2,1,0:T(8,128)(2,1)S(1)}, bf16[12,64,448]{2,1,0:T(8,128)(2,1)}, u32[]{:S(2)}) copy-start(bf16[12,64,448]{2,1,0:T(8,128)(2,1)} %a_ref.1) | copy-start | bytes 2064388
  3.3 1.0 %copy-start.1 = (bf16[12,64,256]{2,1,0:T(8,128)(2,1)S(1)}, bf16[12,64,256]{2,1,0:T(8,128)(2,1)}, u32[]{:S(2)}) copy-start(bf16[12,64,256]{2,1,0:T(8,128)(2,1)} %p_ref.1) | copy-start | bytes 1179652
